TPU v7x, 512 devices: a whole 4x8x8 slice. The times are simulated.
512 devices in a mesh: head: 16 (over y_lo, z), blk: 32 (over y_hi, x, core).
Axes of the slice: x: 4, y: 8 (y_hi: 4, y_lo: 2; y = y_hi * 2 + y_lo), z: 8, core: 2. Of those that a mesh axis runs over, the one named last changes fastest.
Arguments:
- query_rows: bfloat16 [65536, 1024], P(('blk', 'head')), may hold values from -300 to 300
- key_rows: bfloat16 [65536, 1024], P(('blk', 'head')), may hold values from -4 to 4
- value_rows: bfloat16 [65536, 1024], P(('blk', 'head')), may hold values from -6 to 6
- out_grad: bfloat16 [65536, 1024], P(('blk', 'head')), may hold values from -96 to 96
- block_pairs: int32 [512, 8], replicated, may hold values from 0 to 511, as said below
Outputs:
- grad_query: bfloat16 [65536, 1024], P(('blk', 'head'))
- grad_key: bfloat16 [65536, 1024], P(('blk', 'head'))
- grad_value: bfloat16 [65536, 1024], P(('blk', 'head'))
Inputs may be any that keep to these rules, and one draw needn't show every extreme that they name: `block_pairs`: row b names 8 different blocks: b itself first, the others among the blocks of the shard of 2048 tokens that holds b and of the shards just before and after it, counted around a closed loop of all shards.
All inputs are finite; a program needn't handle non-finite values.
Results may differ from a plain program's by a relative error of at most 0.007.
Values may be sent and summed in bfloat16 or wider, within the bound.
A program may use at most 64 MiB of HBM per device.

v0:
```python
import math

import jax
import jax.numpy as jnp
from jax import lax
from jax.sharding import PartitionSpec as P

HEAD_DIM = 64
QB = 128
NNB = 8


def extended(value, sides, width):
    for axis, dim in sides:
        devices, length = (lax.axis_size(axis), value.shape[dim])
        up = [(i, (i + 1) % devices) for i in range(devices)]
        down = [(j, i) for i, j in up]
        last = lax.slice_in_dim(value, length - width, length, axis=dim)
        leading = lax.slice_in_dim(value, 0, width, axis=dim)
        before = lax.ppermute(last, axis, up)
        after = lax.ppermute(leading, axis, down)
        value = jnp.concatenate([before, value, after], axis=dim)
    return value


def shifted(value, axis, by):
    devices = lax.axis_size(axis)
    return lax.ppermute(value, axis, [(i, (i + by) % devices) for i in range(devices)])


def scores_of(q_group, gathered_keys, score_scale):
    return (
        jnp.einsum("gqhd,gkhd->ghqk", q_group, gathered_keys, preferred_element_type=jnp.float32)
        * score_scale
    )


def backward_terms(soft_probs, grad_probs, row_delta, score_scale):
    score_grad = (soft_probs * (grad_probs - row_delta) * score_scale).astype(jnp.bfloat16)
    return (score_grad, soft_probs.astype(jnp.bfloat16))


def key_terms(score_grad, probs_low, q_group, d_group, shape_out):
    part_k = jnp.einsum(
        "ghqk,gqhd->gkhd", score_grad, q_group, preferred_element_type=jnp.float32
    ).reshape(shape_out)
    part_v = jnp.einsum(
        "ghqk,gqhd->gkhd", probs_low, d_group, preferred_element_type=jnp.float32
    ).reshape(shape_out)
    return (part_k, part_v)


def per_device(query_rows, key_rows, value_rows, out_grad, block_pairs):
    score_scale = HEAD_DIM ** (-0.5)
    q_local, k_local, v_local, d_local = (
        lax.all_to_all(query_rows, "head", split_axis=1, concat_axis=0, tiled=True),
        lax.all_to_all(key_rows, "head", split_axis=1, concat_axis=0, tiled=True),
        lax.all_to_all(value_rows, "head", split_axis=1, concat_axis=0, tiled=True),
        lax.all_to_all(out_grad, "head", split_axis=1, concat_axis=0, tiled=True),
    )
    shard_rows = q_local.shape[0]
    feature_width = q_local.shape[1]
    heads_here = feature_width // HEAD_DIM
    per_shard = shard_rows // QB
    cycle_size = lax.axis_size("blk")
    total_blocks = per_shard * cycle_size
    cycle_place = lax.axis_index("blk")
    group_size = math.gcd(per_shard, max(1, 512 // QB))
    step_count = per_shard // group_size
    tile_shape = (group_size, NNB * QB, heads_here, HEAD_DIM)
    part_shape = (group_size * NNB, QB, heads_here, HEAD_DIM)
    stacked_kv = jnp.stack((k_local, v_local), 0)
    kv_window = extended(stacked_kv, (("blk", 1),), shard_rows)
    window_keys = kv_window[0].reshape(3 * per_shard, QB, heads_here, HEAD_DIM)
    window_values = kv_window[1].reshape(3 * per_shard, QB, heads_here, HEAD_DIM)
    own_pairs = lax.dynamic_slice_in_dim(block_pairs, cycle_place * per_shard, per_shard, 0)
    window_ids = (own_pairs - (cycle_place - 1) * per_shard) % total_blocks
    q_blocks = q_local.reshape(step_count, group_size, QB, heads_here, HEAD_DIM)
    d_blocks = d_local.reshape(step_count, group_size, QB, heads_here, HEAD_DIM)
    id_groups = window_ids.reshape(step_count, group_size, NNB)

    def forward_step(running, inputs):
        q_group, d_group, block_ids = inputs
        flat_ids = block_ids.reshape(-1)
        gathered_keys = window_keys[flat_ids].reshape(tile_shape)
        gathered_values = window_values[flat_ids].reshape(tile_shape)
        scores = scores_of(q_group, gathered_keys, score_scale)
        row_top = jnp.max(scores, -1, keepdims=True)
        exp_scores = jnp.exp(scores - row_top)
        row_total = jnp.sum(exp_scores, -1, keepdims=True)
        soft_probs = exp_scores / row_total
        grad_probs = jnp.einsum(
            "gqhd,gkhd->ghqk", d_group, gathered_values, preferred_element_type=jnp.float32
        )
        row_delta = jnp.sum(soft_probs * grad_probs, -1, keepdims=True)
        score_grad, probs_low = backward_terms(soft_probs, grad_probs, row_delta, score_scale)
        grad_q = jnp.einsum(
            "ghqk,gkhd->gqhd", score_grad, gathered_keys, preferred_element_type=jnp.float32
        ).astype(jnp.bfloat16)
        key_acc, value_acc = running
        part_k, part_v = key_terms(score_grad, probs_low, q_group, d_group, part_shape)
        running = (key_acc.at[flat_ids].add(part_k), value_acc.at[flat_ids].add(part_v))
        return (running, (grad_q, row_top[..., 0], row_total[..., 0], row_delta[..., 0]))

    window_zeros = jnp.zeros((3 * per_shard, QB, heads_here, HEAD_DIM), jnp.float32)
    start_acc = (window_zeros, window_zeros)
    (key_acc, value_acc), (grad_q, tops_all, totals_all, deltas_all) = lax.scan(
        forward_step, start_acc, (q_blocks, d_blocks, id_groups)
    )
    grad_q = grad_q.reshape(shard_rows, feature_width)
    partial_sums = jnp.stack((key_acc, value_acc), 0).reshape(2, 3 * shard_rows, feature_width)
    from_right = shifted(partial_sums[:, :shard_rows], "blk", -1)
    from_left = shifted(partial_sums[:, 2 * shard_rows :], "blk", 1)
    grads_kv = partial_sums[:, shard_rows : 2 * shard_rows] + from_right + from_left
    grad_k = grads_kv[0].astype(jnp.bfloat16)
    grad_v = grads_kv[1].astype(jnp.bfloat16)
    return (
        lax.all_to_all(grad_q, "head", split_axis=0, concat_axis=1, tiled=True),
        lax.all_to_all(grad_k, "head", split_axis=0, concat_axis=1, tiled=True),
        lax.all_to_all(grad_v, "head", split_axis=0, concat_axis=1, tiled=True),
    )


def solution(mesh):
    in_specs = (
        P(("blk", "head"), None),
        P(("blk", "head"), None),
        P(("blk", "head"), None),
        P(("blk", "head"), None),
        P(),
    )
    out_specs = (P(("blk", "head"), None), P(("blk", "head"), None), P(("blk", "head"), None))
    return jax.shard_map(
        per_device, mesh=mesh, in_specs=in_specs, out_specs=out_specs, check_vma=False
    )
```

profile of v0, /device:TPU:72, one launch (start us, length us, event | category | flops | bytes accessed | tf_op | source)
XLA Modules:
  0.0 287.2 jit_solution(2495054844425402357)
XLA Ops:
  0.6 1.8 copy.75
  2.4 10.9 %all-to-all-start.1 = ((bf16[128,16,64]{0,2,1:T(8,128)(2,1)}), bf16[128,16,64]{0,2,1:T(8,128)(2,1)S(1)}, u32[]{:S(2)}, u32[]{:S(2)}) async-start(bf16[128,16,64]{0,2,1:T(8,128)(2,1)} %bitcast.21), calls=%async_computation.1 | async-start | bytes 524288 | tf_op jit(solution)/shard_map/all_to_all | solution.py:57
  13.3 1.8 copy.77
  15.2 8.3 %all-to-all-done.1 = bf16[128,16,64]{0,2,1:T(8,128)(2,1)S(1)} async-done(((bf16[128,16,64]{0,2,1:T(8,128)(2,1)}), bf16[128,16,64]{0,2,1:T(8,128)(2,1)S(1)}, u32[]{:S(2)}, u32[]{:S(2)}) %all-to-all-start.1) | async-done | bytes 262176 | tf_op jit(solution)/shard_map/all_to_all | solution.py:57
  23.5 4.5 %all-to-all-start.2 = ((bf16[128,16,64]{0,2,1:T(8,128)(2,1)}), bf16[128,16,64]{0,2,1:T(8,128)(2,1)S(1)}, u32[]{:S(2)}, u32[]{:S(2)}) async-start(bf16[128,16,64]{0,2,1:T(8,128)(2,1)} %bitcast.23), calls=%async_computation.2 | async-start | bytes 524288 | tf_op jit(solution)/shard_map/all_to_all | solution.py:58
  28.3 10.0 %all-to-all-done.2 = bf16[128,16,64]{0,2,1:T(8,128)(2,1)S(1)} async-done(((bf16[128,16,64]{0,2,1:T(8,128)(2,1)}), bf16[128,16,64]{0,2,1:T(8,128)(2,1)S(1)}, u32[]{:S(2)}, u32[]{:S(2)}) %all-to-all-start.2) | async-done | bytes 262176 | tf_op jit(solution)/shard_map/all_to_all | solution.py:58
  38.6 6.7 %collective-permute-start.1 = (bf16[2,2048,64]{1,2,0:T(8,128)(2,1)S(1)}, bf16[2,2048,64]{1,2,0:T(8,128)(2,1)S(1)}, u32[]{:S(2)}, u32[]{:S(2)}) collective-permute-start(bf16[2,2048,64]{1,2,0:T(8,128)(2,1)S(1)} %constant_dynamic-update-slice_fusion), channel_id=1, source_target_pairs={{1,0},{2,1},{3,2},{4,3},{5,4},{6,5},{7,6},{8,7},{9,8},{10,9},{11,1... | collective-permute-start | bytes 1572872 | tf_op jit(solution)/shard_map/ppermute | solution.py:21
  45.3 1.9 collective-permute-start
  47.3 0.8 copy.74
  48.1 4.8 %all-to-all-start = ((bf16[128,16,64]{0,2,1:T(8,128)(2,1)}), bf16[128,16,64]{0,2,1:T(8,128)(2,1)S(1)}, u32[]{:S(2)}, u32[]{:S(2)}) async-start(bf16[128,16,64]{0,2,1:T(8,128)(2,1)} %bitcast.17), calls=%async_computation | async-start | bytes 524288 | tf_op jit(solution)/shard_map/all_to_all | solution.py:56
  53.1 0.8 copy.79
  54.0 7.7 %all-to-all-done = bf16[128,16,64]{0,2,1:T(8,128)(2,1)S(1)} async-done(((bf16[128,16,64]{0,2,1:T(8,128)(2,1)}), bf16[128,16,64]{0,2,1:T(8,128)(2,1)S(1)}, u32[]{:S(2)}, u32[]{:S(2)}) %all-to-all-start) | async-done | bytes 262176 | tf_op jit(solution)/shard_map/all_to_all | solution.py:56
  61.7 5.5 %all-to-all-start.3 = ((bf16[128,16,64]{0,2,1:T(8,128)(2,1)}), bf16[128,16,64]{0,2,1:T(8,128)(2,1)S(1)}, u32[]{:S(2)}, u32[]{:S(2)}) async-start(bf16[128,16,64]{0,2,1:T(8,128)(2,1)} %bitcast.25), calls=%async_computation.3 | async-start | bytes 524288 | tf_op jit(solution)/shard_map/all_to_all | solution.py:59
  68.1 7.9 %all-to-all-done.3 = bf16[128,16,64]{0,2,1:T(8,128)(2,1)S(1)} async-done(((bf16[128,16,64]{0,2,1:T(8,128)(2,1)}), bf16[128,16,64]{0,2,1:T(8,128)(2,1)S(1)}, u32[]{:S(2)}, u32[]{:S(2)}) %all-to-all-start.3) | async-done | bytes 262176 | tf_op jit(solution)/shard_map/all_to_all | solution.py:59
  76.0 1.3 broadcast_in_dim.7.clone
  77.3 1.3 broadcast_in_dim.7
  78.7 125.6 %while.14 = (s32[]{:T(128)}, f32[48,128,1,64]{1,3,0,2:T(8,128)}, f32[48,128,1,64]{1,3,0,2:T(8,128)}, bf16[4,4,128,1,64]{2,4,1,3,0:T(8,128)(2,1)}, s32[4,4,8]{2,1...) while((s32[]{:T(128)}, f32[48,128,1,64]{1,3,0,2:T(8,128)}, ...), condition=%wide.region_6.7_spmd, body=%wide.region_0.6_spmd.sunk | while | flops 346068064 | bytes 66930348 | solution.py:107
  81.6 3.0 %fusion.105 = (f32[4,128]{1,0:T(4,128)S(1)}, f32[4,128,1024]{2,1,0:T(8,128)}) fusion(bf16[4,1024,64]{1,0,2:T(4,128)(2,1)S(1)} %reshape.222, bf16[4,4,128,1,64]{2,4,1,3,0:T(8,128)(2,1)} %copy-done.7, s32[]{:T(128)S(6)} %copy.138), kind=kOutput, calls=%fused_computation.77.clone.1 | convolution fusion | flops 68682752 | bytes 2689028 | tf_op jit(solution)/shard_map/while/body/eval_jaxpr/sub | solution.py:89
  84.6 5.4 %fusion.107 = bf16[4,4,128,1,64]{2,4,1,3,0:T(8,128)(2,1)} fusion(bf16[4,4,128,1,64]{2,4,1,3,0:T(8,128)(2,1)} %get-tuple-element.189, s32[]{:T(128)S(6)} %copy.138, f32[4,128,1024]{2,1,0:T(8,128)S(1)} %fusion.104, bf16[4,1024,64]{1,0,2:T(4,128)(2,1)S(1)} %reshape.222, f32[4,128,1024]{2,1,0:T(8,128)} %get-tuple-element.174, ...), kind=kOutput, calls=%fused_computation.18.clone.1 | convolution fusion | flops 70813184 | bytes 8982532 | tf_op jit(solution)/shard_map/while/body/eval_jaxpr/ghqk,gkhd->gqhd/dot_general | solution.py:97
  90.0 4.9 %fusion.106 = f32[4,1024,1,64]{1,3,0,2:T(8,128)S(1)} fusion(f32[4,128,1024]{2,1,0:T(8,128)S(1)} %fusion.104, bf16[4,4,128,1,64]{2,4,1,3,0:T(8,128)(2,1)} %copy-done.7, s32[]{:T(128)S(6)} %copy.138, f32[4,128,1024]{2,1,0:T(8,128)} %get-tuple-element.174, f32[4,128]{1,0:T(4,128)S(1)} %get-tuple-element.175), kind=kOutput, calls=%fused_computation.14.clone.1 | convolution fusion | flops 70780416 | bytes 9506820 | tf_op jit(solution)/shard_map/while/body/eval_jaxpr/ghqk,gqhd->gkhd/dot_general | solution.py:44
  94.9 2.0 convolution_bitcast_fusion.2
  96.8 0.7 copy.128
  98.6 0.7 copy.126
  100.3 4.8 %scatter_fusion = f32[48,128,64]{1,2,0:T(8,128)} fusion(f32[48,128,64]{1,2,0:T(8,128)} %bitcast.128, s32[32]{0:T(128)S(1)} %fusion.103, f32[32,128,64]{1,2,0:T(8,128)S(1)} %copy.127), kind=kCustom, calls=%fused_computation.2.clone.1 | custom fusion | flops 262144 | bytes 3145856 | tf_op jit(solution)/shard_map/while/body/eval_jaxpr/scatter-add | solution.py:102
  105.1 4.8 %scatter_fusion.1 = f32[48,128,64]{1,2,0:T(8,128)} fusion(f32[48,128,64]{1,2,0:T(8,128)} %bitcast.132, s32[32]{0:T(128)S(1)} %fusion.103, f32[32,128,64]{1,2,0:T(8,128)S(1)} %copy.129), kind=kCustom, calls=%fused_computation.3.clone.1 | custom fusion | flops 262144 | bytes 3145856 | tf_op jit(solution)/shard_map/while/body/eval_jaxpr/scatter-add | solution.py:102
  112.9 3.0 %fusion.105 = (f32[4,128]{1,0:T(4,128)S(1)}, f32[4,128,1024]{2,1,0:T(8,128)}) fusion(bf16[4,1024,64]{1,0,2:T(4,128)(2,1)S(1)} %reshape.222, bf16[4,4,128,1,64]{2,4,1,3,0:T(8,128)(2,1)} %copy-done.7, s32[]{:T(128)S(6)} %copy.138), kind=kOutput, calls=%fused_computation.77.clone.1 | convolution fusion | flops 68682752 | bytes 2689028 | tf_op jit(solution)/shard_map/while/body/eval_jaxpr/sub | solution.py:89
  115.9 5.4 %fusion.107 = bf16[4,4,128,1,64]{2,4,1,3,0:T(8,128)(2,1)} fusion(bf16[4,4,128,1,64]{2,4,1,3,0:T(8,128)(2,1)} %get-tuple-element.189, s32[]{:T(128)S(6)} %copy.138, f32[4,128,1024]{2,1,0:T(8,128)S(1)} %fusion.104, bf16[4,1024,64]{1,0,2:T(4,128)(2,1)S(1)} %reshape.222, f32[4,128,1024]{2,1,0:T(8,128)} %get-tuple-element.174, ...), kind=kOutput, calls=%fused_computation.18.clone.1 | convolution fusion | flops 70813184 | bytes 8982532 | tf_op jit(solution)/shard_map/while/body/eval_jaxpr/ghqk,gkhd->gqhd/dot_general | solution.py:97
  121.3 4.9 %fusion.106 = f32[4,1024,1,64]{1,3,0,2:T(8,128)S(1)} fusion(f32[4,128,1024]{2,1,0:T(8,128)S(1)} %fusion.104, bf16[4,4,128,1,64]{2,4,1,3,0:T(8,128)(2,1)} %copy-done.7, s32[]{:T(128)S(6)} %copy.138, f32[4,128,1024]{2,1,0:T(8,128)} %get-tuple-element.174, f32[4,128]{1,0:T(4,128)S(1)} %get-tuple-element.175), kind=kOutput, calls=%fused_computation.14.clone.1 | convolution fusion | flops 70780416 | bytes 9506820 | tf_op jit(solution)/shard_map/while/body/eval_jaxpr/ghqk,gqhd->gkhd/dot_general | solution.py:44
  126.2 2.0 convolution_bitcast_fusion.2
  128.1 0.7 copy.128
  129.9 0.7 copy.126
  131.6 4.8 %scatter_fusion = f32[48,128,64]{1,2,0:T(8,128)} fusion(f32[48,128,64]{1,2,0:T(8,128)} %bitcast.128, s32[32]{0:T(128)S(1)} %fusion.103, f32[32,128,64]{1,2,0:T(8,128)S(1)} %copy.127), kind=kCustom, calls=%fused_computation.2.clone.1 | custom fusion | flops 262144 | bytes 3145856 | tf_op jit(solution)/shard_map/while/body/eval_jaxpr/scatter-add | solution.py:102
  136.4 4.8 %scatter_fusion.1 = f32[48,128,64]{1,2,0:T(8,128)} fusion(f32[48,128,64]{1,2,0:T(8,128)} %bitcast.132, s32[32]{0:T(128)S(1)} %fusion.103, f32[32,128,64]{1,2,0:T(8,128)S(1)} %copy.129), kind=kCustom, calls=%fused_computation.3.clone.1 | custom fusion | flops 262144 | bytes 3145856 | tf_op jit(solution)/shard_map/while/body/eval_jaxpr/scatter-add | solution.py:102
  144.2 3.0 %fusion.105 = (f32[4,128]{1,0:T(4,128)S(1)}, f32[4,128,1024]{2,1,0:T(8,128)}) fusion(bf16[4,1024,64]{1,0,2:T(4,128)(2,1)S(1)} %reshape.222, bf16[4,4,128,1,64]{2,4,1,3,0:T(8,128)(2,1)} %copy-done.7, s32[]{:T(128)S(6)} %copy.138), kind=kOutput, calls=%fused_computation.77.clone.1 | convolution fusion | flops 68682752 | bytes 2689028 | tf_op jit(solution)/shard_map/while/body/eval_jaxpr/sub | solution.py:89
  147.3 5.4 %fusion.107 = bf16[4,4,128,1,64]{2,4,1,3,0:T(8,128)(2,1)} fusion(bf16[4,4,128,1,64]{2,4,1,3,0:T(8,128)(2,1)} %get-tuple-element.189, s32[]{:T(128)S(6)} %copy.138, f32[4,128,1024]{2,1,0:T(8,128)S(1)} %fusion.104, bf16[4,1024,64]{1,0,2:T(4,128)(2,1)S(1)} %reshape.222, f32[4,128,1024]{2,1,0:T(8,128)} %get-tuple-element.174, ...), kind=kOutput, calls=%fused_computation.18.clone.1 | convolution fusion | flops 70813184 | bytes 8982532 | tf_op jit(solution)/shard_map/while/body/eval_jaxpr/ghqk,gkhd->gqhd/dot_general | solution.py:97
  152.6 4.9 %fusion.106 = f32[4,1024,1,64]{1,3,0,2:T(8,128)S(1)} fusion(f32[4,128,1024]{2,1,0:T(8,128)S(1)} %fusion.104, bf16[4,4,128,1,64]{2,4,1,3,0:T(8,128)(2,1)} %copy-done.7, s32[]{:T(128)S(6)} %copy.138, f32[4,128,1024]{2,1,0:T(8,128)} %get-tuple-element.174, f32[4,128]{1,0:T(4,128)S(1)} %get-tuple-element.175), kind=kOutput, calls=%fused_computation.14.clone.1 | convolution fusion | flops 70780416 | bytes 9506820 | tf_op jit(solution)/shard_map/while/body/eval_jaxpr/ghqk,gqhd->gkhd/dot_general | solution.py:44
  157.5 2.0 convolution_bitcast_fusion.2
  162.9 4.9 %scatter_fusion = f32[48,128,64]{1,2,0:T(8,128)} fusion(f32[48,128,64]{1,2,0:T(8,128)} %bitcast.128, s32[32]{0:T(128)S(1)} %fusion.103, f32[32,128,64]{1,2,0:T(8,128)S(1)} %copy.127), kind=kCustom, calls=%fused_computation.2.clone.1 | custom fusion | flops 262144 | bytes 3145856 | tf_op jit(solution)/shard_map/while/body/eval_jaxpr/scatter-add | solution.py:102
  167.9 4.9 %scatter_fusion.1 = f32[48,128,64]{1,2,0:T(8,128)} fusion(f32[48,128,64]{1,2,0:T(8,128)} %bitcast.132, s32[32]{0:T(128)S(1)} %fusion.103, f32[32,128,64]{1,2,0:T(8,128)S(1)} %copy.129), kind=kCustom, calls=%fused_computation.3.clone.1 | custom fusion | flops 262144 | bytes 3145856 | tf_op jit(solution)/shard_map/while/body/eval_jaxpr/scatter-add | solution.py:102
  175.7 3.0 %fusion.105 = (f32[4,128]{1,0:T(4,128)S(1)}, f32[4,128,1024]{2,1,0:T(8,128)}) fusion(bf16[4,1024,64]{1,0,2:T(4,128)(2,1)S(1)} %reshape.222, bf16[4,4,128,1,64]{2,4,1,3,0:T(8,128)(2,1)} %copy-done.7, s32[]{:T(128)S(6)} %copy.138), kind=kOutput, calls=%fused_computation.77.clone.1 | convolution fusion | flops 68682752 | bytes 2689028 | tf_op jit(solution)/shard_map/while/body/eval_jaxpr/sub | solution.py:89
  178.7 5.4 %fusion.107 = bf16[4,4,128,1,64]{2,4,1,3,0:T(8,128)(2,1)} fusion(bf16[4,4,128,1,64]{2,4,1,3,0:T(8,128)(2,1)} %get-tuple-element.189, s32[]{:T(128)S(6)} %copy.138, f32[4,128,1024]{2,1,0:T(8,128)S(1)} %fusion.104, bf16[4,1024,64]{1,0,2:T(4,128)(2,1)S(1)} %reshape.222, f32[4,128,1024]{2,1,0:T(8,128)} %get-tuple-element.174, ...), kind=kOutput, calls=%fused_computation.18.clone.1 | convolution fusion | flops 70813184 | bytes 8982532 | tf_op jit(solution)/shard_map/while/body/eval_jaxpr/ghqk,gkhd->gqhd/dot_general | solution.py:97
  184.1 4.9 %fusion.106 = f32[4,1024,1,64]{1,3,0,2:T(8,128)S(1)} fusion(f32[4,128,1024]{2,1,0:T(8,128)S(1)} %fusion.104, bf16[4,4,128,1,64]{2,4,1,3,0:T(8,128)(2,1)} %copy-done.7, s32[]{:T(128)S(6)} %copy.138, f32[4,128,1024]{2,1,0:T(8,128)} %get-tuple-element.174, f32[4,128]{1,0:T(4,128)S(1)} %get-tuple-element.175), kind=kOutput, calls=%fused_computation.14.clone.1 | convolution fusion | flops 70780416 | bytes 9506820 | tf_op jit(solution)/shard_map/while/body/eval_jaxpr/ghqk,gqhd->gkhd/dot_general | solution.py:44
  189.0 2.0 convolution_bitcast_fusion.2
  194.4 4.8 %scatter_fusion = f32[48,128,64]{1,2,0:T(8,128)} fusion(f32[48,128,64]{1,2,0:T(8,128)} %bitcast.128, s32[32]{0:T(128)S(1)} %fusion.103, f32[32,128,64]{1,2,0:T(8,128)S(1)} %copy.127), kind=kCustom, calls=%fused_computation.2.clone.1 | custom fusion | flops 262144 | bytes 3145856 | tf_op jit(solution)/shard_map/while/body/eval_jaxpr/scatter-add | solution.py:102
  199.2 4.8 %scatter_fusion.1 = f32[48,128,64]{1,2,0:T(8,128)} fusion(f32[48,128,64]{1,2,0:T(8,128)} %bitcast.132, s32[32]{0:T(128)S(1)} %fusion.103, f32[32,128,64]{1,2,0:T(8,128)S(1)} %copy.129), kind=kCustom, calls=%fused_computation.3.clone.1 | custom fusion | flops 262144 | bytes 3145856 | tf_op jit(solution)/shard_map/while/body/eval_jaxpr/scatter-add | solution.py:102
  204.3 2.3 copy.84
  206.6 2.3 copy.85
  208.9 2.9 %fusion.65 = (f32[2,2048,64]{1,0,2:T(2,128)}, f32[2,2048,64]{1,0,2:T(2,128)}) fusion(f32[1,6144,64]{1,0,2:T(1,128)S(1)} %bitcast.136, f32[1,6144,64]{1,0,2:T(1,128)S(1)} %bitcast.138), kind=kLoop, calls=%fused_computation.58 | loop fusion | flops 524288 | bytes 5242880 | tf_op jit(solution)/shard_map/stack | solution.py:111
  211.8 9.8 %collective-permute-start.2 = (f32[2,2048,64]{1,0,2:T(2,128)}, f32[2,2048,64]{1,0,2:T(2,128)}, u32[]{:S(2)}, u32[]{:S(2)}) collective-permute-start(f32[2,2048,64]{1,0,2:T(2,128)} %get-tuple-element.113), channel_id=1, source_target_pairs={{0,31},{1,0},{2,1},{3,2},{4,3},{5,4},{6,5},{7,6},{8,7},{9,8},{10,9... | collective-permute-start | bytes 3145736 | tf_op jit(solution)/shard_map/ppermute | solution.py:28
  221.6 1.9 collective-permute-start.3
  223.6 4.7 %all-to-all-start.4 = ((bf16[16,128,64]{1,2,0:T(8,128)(2,1)}), bf16[16,128,64]{1,2,0:T(8,128)(2,1)S(1)}, u32[]{:S(2)}, u32[]{:S(2)}) async-start(bf16[16,128,64]{1,2,0:T(8,128)(2,1)} %bitcast.29), calls=%async_computation.4 | async-start | bytes 524288 | tf_op jit(solution)/shard_map/all_to_all | solution.py:118
  228.3 16.1 %collective-permute-done.2 = f32[2,2048,64]{1,0,2:T(2,128)} collective-permute-done((f32[2,2048,64]{1,0,2:T(2,128)}, f32[2,2048,64]{1,0,2:T(2,128)}, u32[]{:S(2)}, u32[]{:S(2)}) %collective-permute-start.2) | collective-permute-done | bytes 1048608 | tf_op jit(solution)/shard_map/ppermute | solution.py:28
  244.4 1.5 collective-permute-done.3
  245.9 2.9 %fusion.69 = bf16[2,2048,64]{1,0,2:T(2,128)(2,1)S(1)} fusion(f32[2,2048,64]{1,0,2:T(2,128)} %collective-permute-done.3, f32[2,2048,64]{1,0,2:T(2,128)} %collective-permute-done.2, f32[1,6144,64]{1,0,2:T(1,128)S(1)} %bitcast.139, f32[1,6144,64]{1,0,2:T(1,128)S(1)} %bitcast.137), kind=kLoop, calls=%fused_computation.63 | loop fusion | flops 1048576 | bytes 5767168 | tf_op jit(solution)/shard_map/convert.1
  248.8 2.2 slice_reduce_fusion
  251.0 0.8 copy_bitcast_fusion
  251.7 12.7 %all-to-all-start.6 = ((bf16[16,128,64]{1,2,0:T(8,128)(2,1)}), bf16[16,128,64]{1,2,0:T(8,128)(2,1)S(1)}, u32[]{:S(2)}, u32[]{:S(2)}) async-start(bf16[16,128,64]{1,2,0:T(8,128)(2,1)} %copy_bitcast_fusion), calls=%async_computation.6 | async-start | bytes 524288 | tf_op jit(solution)/shard_map/all_to_all | solution.py:120
  264.4 0.8 copy_bitcast_fusion.1
  265.2 7.9 %all-to-all-done.6 = bf16[16,128,64]{1,2,0:T(8,128)(2,1)S(1)} async-done(((bf16[16,128,64]{1,2,0:T(8,128)(2,1)}), bf16[16,128,64]{1,2,0:T(8,128)(2,1)S(1)}, u32[]{:S(2)}, u32[]{:S(2)}) %all-to-all-start.6) | async-done | bytes 262176 | tf_op jit(solution)/shard_map/all_to_all | solution.py:120
  273.1 4.6 %all-to-all-start.5 = ((bf16[16,128,64]{1,2,0:T(8,128)(2,1)}), bf16[16,128,64]{1,2,0:T(8,128)(2,1)S(1)}, u32[]{:S(2)}, u32[]{:S(2)}) async-start(bf16[16,128,64]{1,2,0:T(8,128)(2,1)} %copy_bitcast_fusion.1), calls=%async_computation.5 | async-start | bytes 524288 | tf_op jit(solution)/shard_map/all_to_all | solution.py:119
  277.7 0.8 copy.88
  278.5 0.8 copy.90
  279.4 7.0 %all-to-all-done.5 = bf16[16,128,64]{1,2,0:T(8,128)(2,1)S(1)} async-done(((bf16[16,128,64]{1,2,0:T(8,128)(2,1)}), bf16[16,128,64]{1,2,0:T(8,128)(2,1)S(1)}, u32[]{:S(2)}, u32[]{:S(2)}) %all-to-all-start.5) | async-done | bytes 262176 | tf_op jit(solution)/shard_map/all_to_all | solution.py:119
  286.4 0.8 copy.89
  (137 shorter events, 24.0 us)
Async XLA Ops:
  0.6 52.3 %copy-start = (s32[512,8]{0,1:T(8,128)S(1)}, s32[512,8]{0,1:T(8,128)}, u32[]{:S(2)}) copy-start(s32[512,8]{0,1:T(8,128)} %param.11) | copy-start | bytes 49156
  2.4 21.0 %all-to-all-start.1 = ((bf16[128,16,64]{0,2,1:T(8,128)(2,1)}), bf16[128,16,64]{0,2,1:T(8,128)(2,1)S(1)}, u32[]{:S(2)}, u32[]{:S(2)}) async-start(bf16[128,16,64]{0,2,1:T(8,128)(2,1)} %bitcast.21), calls=%async_computation.1 | async-start | bytes 524288 | tf_op jit(solution)/shard_map/all_to_all | solution.py:57
  13.3 33.9 %copy-start.5 = (bf16[128,1024]{1,0:T(8,128)(2,1)S(1)}, bf16[128,1024]{1,0:T(8,128)(2,1)}, u32[]{:S(2)}) copy-start(bf16[128,1024]{1,0:T(8,128)(2,1)} %param.7) | copy-start | bytes 786436
  23.5 14.8 %all-to-all-start.2 = ((bf16[128,16,64]{0,2,1:T(8,128)(2,1)}), bf16[128,16,64]{0,2,1:T(8,128)(2,1)S(1)}, u32[]{:S(2)}, u32[]{:S(2)}) async-start(bf16[128,16,64]{0,2,1:T(8,128)(2,1)} %bitcast.23), calls=%async_computation.2 | async-start | bytes 524288 | tf_op jit(solution)/shard_map/all_to_all | solution.py:58
  28.0 25.2 %copy-start.6 = (bf16[128,1024]{1,0:T(8,128)(2,1)S(1)}, bf16[128,1024]{1,0:T(8,128)(2,1)}, u32[]{:S(2)}) copy-start(bf16[128,1024]{1,0:T(8,128)(2,1)} %param.10) | copy-start | bytes 786436
  38.6 28.5 %collective-permute-start.1 = (bf16[2,2048,64]{1,2,0:T(8,128)(2,1)S(1)}, bf16[2,2048,64]{1,2,0:T(8,128)(2,1)S(1)}, u32[]{:S(2)}, u32[]{:S(2)}) collective-permute-start(bf16[2,2048,64]{1,2,0:T(8,128)(2,1)S(1)} %constant_dynamic-update-slice_fusion), channel_id=1, source_target_pairs={{1,0},{2,1},{3,2},{4,3},{5,4},{6,5},{7,6},{8,7},{9,8},{10,9},{11,1... | collective-permute-start | bytes 1572872 | tf_op jit(solution)/shard_map/ppermute | solution.py:21
  45.3 21.8 %collective-permute-start = (bf16[2,2048,64]{1,2,0:T(8,128)(2,1)S(1)}, bf16[2,2048,64]{1,2,0:T(8,128)(2,1)S(1)}, u32[]{:S(2)}, u32[]{:S(2)}) collective-permute-start(bf16[2,2048,64]{1,2,0:T(8,128)(2,1)S(1)} %constant_dynamic-update-slice_fusion), channel_id=1, source_target_pairs={{0,1},{1,2},{2,3},{3,4},{4,5},{5,6},{6,7},{7,8},{8,9},{9,10},{10,1... | collective-permute-start | bytes 1572872 | tf_op jit(solution)/shard_map/ppermute | solution.py:20
  48.1 13.6 %all-to-all-start = ((bf16[128,16,64]{0,2,1:T(8,128)(2,1)}), bf16[128,16,64]{0,2,1:T(8,128)(2,1)S(1)}, u32[]{:S(2)}, u32[]{:S(2)}) async-start(bf16[128,16,64]{0,2,1:T(8,128)(2,1)} %bitcast.17), calls=%async_computation | async-start | bytes 524288 | tf_op jit(solution)/shard_map/all_to_all | solution.py:56
  61.7 14.3 %all-to-all-start.3 = ((bf16[128,16,64]{0,2,1:T(8,128)(2,1)}), bf16[128,16,64]{0,2,1:T(8,128)(2,1)S(1)}, u32[]{:S(2)}, u32[]{:S(2)}) async-start(bf16[128,16,64]{0,2,1:T(8,128)(2,1)} %bitcast.25), calls=%async_computation.3 | async-start | bytes 524288 | tf_op jit(solution)/shard_map/all_to_all | solution.py:59
  78.7 0.8 copy-start.7
  78.7 1.3 copy-start.1
  78.7 1.3 copy-start.3
  105.1 4.8 %copy-start.2 = (bf16[48,128,1,64]{1,3,2,0:T(8,128)(2,1)S(1)}, bf16[48,128,1,64]{1,3,2,0:T(8,128)(2,1)}, u32[]{:S(2)}) copy-start(bf16[48,128,1,64]{1,3,2,0:T(8,128)(2,1)} %copy-done.1) | copy-start | bytes 2359300 | tf_op jit(solution)/shard_map/while
  105.1 4.8 %copy-start.4 = (bf16[48,128,1,64]{1,3,2,0:T(8,128)(2,1)S(1)}, bf16[48,128,1,64]{1,3,2,0:T(8,128)(2,1)}, u32[]{:S(2)}) copy-start(bf16[48,128,1,64]{1,3,2,0:T(8,128)(2,1)} %copy-done.3) | copy-start | bytes 2359300 | tf_op jit(solution)/shard_map/while
  105.1 4.8 %copy-start.8 = (bf16[4,4,128,1,64]{2,4,1,3,0:T(8,128)(2,1)S(1)}, bf16[4,4,128,1,64]{2,4,1,3,0:T(8,128)(2,1)}, u32[]{:S(2)}) copy-start(bf16[4,4,128,1,64]{2,4,1,3,0:T(8,128)(2,1)} %copy-done.7) | copy-start | bytes 786436 | tf_op jit(solution)/shard_map/while
  109.9 0.8 copy-start.7
  110.0 1.3 copy-start.1
  110.0 1.3 copy-start.3
  136.4 4.8 %copy-start.2 = (bf16[48,128,1,64]{1,3,2,0:T(8,128)(2,1)S(1)}, bf16[48,128,1,64]{1,3,2,0:T(8,128)(2,1)}, u32[]{:S(2)}) copy-start(bf16[48,128,1,64]{1,3,2,0:T(8,128)(2,1)} %copy-done.1) | copy-start | bytes 2359300 | tf_op jit(solution)/shard_map/while
  136.4 4.8 %copy-start.4 = (bf16[48,128,1,64]{1,3,2,0:T(8,128)(2,1)S(1)}, bf16[48,128,1,64]{1,3,2,0:T(8,128)(2,1)}, u32[]{:S(2)}) copy-start(bf16[48,128,1,64]{1,3,2,0:T(8,128)(2,1)} %copy-done.3) | copy-start | bytes 2359300 | tf_op jit(solution)/shard_map/while
  136.4 4.8 %copy-start.8 = (bf16[4,4,128,1,64]{2,4,1,3,0:T(8,128)(2,1)S(1)}, bf16[4,4,128,1,64]{2,4,1,3,0:T(8,128)(2,1)}, u32[]{:S(2)}) copy-start(bf16[4,4,128,1,64]{2,4,1,3,0:T(8,128)(2,1)} %copy-done.7) | copy-start | bytes 786436 | tf_op jit(solution)/shard_map/while
  141.3 0.8 copy-start.7
  141.3 1.3 copy-start.1
  141.3 1.3 copy-start.3
  167.8 4.9 %copy-start.2 = (bf16[48,128,1,64]{1,3,2,0:T(8,128)(2,1)S(1)}, bf16[48,128,1,64]{1,3,2,0:T(8,128)(2,1)}, u32[]{:S(2)}) copy-start(bf16[48,128,1,64]{1,3,2,0:T(8,128)(2,1)} %copy-done.1) | copy-start | bytes 2359300 | tf_op jit(solution)/shard_map/while
  167.8 4.9 %copy-start.4 = (bf16[48,128,1,64]{1,3,2,0:T(8,128)(2,1)S(1)}, bf16[48,128,1,64]{1,3,2,0:T(8,128)(2,1)}, u32[]{:S(2)}) copy-start(bf16[48,128,1,64]{1,3,2,0:T(8,128)(2,1)} %copy-done.3) | copy-start | bytes 2359300 | tf_op jit(solution)/shard_map/while
  167.8 4.9 %copy-start.8 = (bf16[4,4,128,1,64]{2,4,1,3,0:T(8,128)(2,1)S(1)}, bf16[4,4,128,1,64]{2,4,1,3,0:T(8,128)(2,1)}, u32[]{:S(2)}) copy-start(bf16[4,4,128,1,64]{2,4,1,3,0:T(8,128)(2,1)} %copy-done.7) | copy-start | bytes 786436 | tf_op jit(solution)/shard_map/while
  172.7 0.8 copy-start.7
  172.8 1.3 copy-start.1
  172.8 1.3 copy-start.3
  199.2 4.8 %copy-start.2 = (bf16[48,128,1,64]{1,3,2,0:T(8,128)(2,1)S(1)}, bf16[48,128,1,64]{1,3,2,0:T(8,128)(2,1)}, u32[]{:S(2)}) copy-start(bf16[48,128,1,64]{1,3,2,0:T(8,128)(2,1)} %copy-done.1) | copy-start | bytes 2359300 | tf_op jit(solution)/shard_map/while
  199.2 4.8 %copy-start.4 = (bf16[48,128,1,64]{1,3,2,0:T(8,128)(2,1)S(1)}, bf16[48,128,1,64]{1,3,2,0:T(8,128)(2,1)}, u32[]{:S(2)}) copy-start(bf16[48,128,1,64]{1,3,2,0:T(8,128)(2,1)} %copy-done.3) | copy-start | bytes 2359300 | tf_op jit(solution)/shard_map/while
  199.2 4.8 %copy-start.8 = (bf16[4,4,128,1,64]{2,4,1,3,0:T(8,128)(2,1)S(1)}, bf16[4,4,128,1,64]{2,4,1,3,0:T(8,128)(2,1)}, u32[]{:S(2)}) copy-start(bf16[4,4,128,1,64]{2,4,1,3,0:T(8,128)(2,1)} %copy-done.7) | copy-start | bytes 786436 | tf_op jit(solution)/shard_map/while
  211.8 32.6 %collective-permute-start.2 = (f32[2,2048,64]{1,0,2:T(2,128)}, f32[2,2048,64]{1,0,2:T(2,128)}, u32[]{:S(2)}, u32[]{:S(2)}) collective-permute-start(f32[2,2048,64]{1,0,2:T(2,128)} %get-tuple-element.113), channel_id=1, source_target_pairs={{0,31},{1,0},{2,1},{3,2},{4,3},{5,4},{6,5},{7,6},{8,7},{9,8},{10,9... | collective-permute-start | bytes 3145736 | tf_op jit(solution)/shard_map/ppermute | solution.py:28
  221.6 24.2 %collective-permute-start.3 = (f32[2,2048,64]{1,0,2:T(2,128)}, f32[2,2048,64]{1,0,2:T(2,128)}, u32[]{:S(2)}, u32[]{:S(2)}) collective-permute-start(f32[2,2048,64]{1,0,2:T(2,128)} %get-tuple-element.114), channel_id=1, source_target_pairs={{0,1},{1,2},{2,3},{3,4},{4,5},{5,6},{6,7},{7,8},{8,9},{9,10},{10,1... | collective-permute-start | bytes 3145736 | tf_op jit(solution)/shard_map/ppermute | solution.py:28
  223.6 28.2 %all-to-all-start.4 = ((bf16[16,128,64]{1,2,0:T(8,128)(2,1)}), bf16[16,128,64]{1,2,0:T(8,128)(2,1)S(1)}, u32[]{:S(2)}, u32[]{:S(2)}) async-start(bf16[16,128,64]{1,2,0:T(8,128)(2,1)} %bitcast.29), calls=%async_computation.4 | async-start | bytes 524288 | tf_op jit(solution)/shard_map/all_to_all | solution.py:118
  251.7 21.4 %all-to-all-start.6 = ((bf16[16,128,64]{1,2,0:T(8,128)(2,1)}), bf16[16,128,64]{1,2,0:T(8,128)(2,1)S(1)}, u32[]{:S(2)}, u32[]{:S(2)}) async-start(bf16[16,128,64]{1,2,0:T(8,128)(2,1)} %copy_bitcast_fusion), calls=%async_computation.6 | async-start | bytes 524288 | tf_op jit(solution)/shard_map/all_to_all | solution.py:120
  273.1 13.2 %all-to-all-start.5 = ((bf16[16,128,64]{1,2,0:T(8,128)(2,1)}), bf16[16,128,64]{1,2,0:T(8,128)(2,1)S(1)}, u32[]{:S(2)}, u32[]{:S(2)}) async-start(bf16[16,128,64]{1,2,0:T(8,128)(2,1)} %copy_bitcast_fusion.1), calls=%async_computation.5 | async-start | bytes 524288 | tf_op jit(solution)/shard_map/all_to_all | solution.py:119
where the time goes:
time: 290 us; the launch traced here: 287 us
  starting transfers between devices  68 us (23%)
  waiting for transfers between devices  66.5 us (23%)
  matrix products  62.9 us (22%)
  other arithmetic  44.6 us (15%)
  local copies, waits for them, and re-layouts  43.5 us (15%)
    dot_general x4, matrix products, forward_step(): jnp.einsum('ghqk,gkhd->gqhd', score_grad, gathered_keys, preferred_elemen...  21.5 us
    dot_general x4, matrix products, key_terms(): jnp.einsum('ghqk,gqhd->gkhd', score_grad, q_group, preferred_element_type...  19.5 us
    scatter-add x4, other arithmetic, forward_step(): key_acc.at[flat_ids].add(part_k)  19.4 us
    scatter-add x4, other arithmetic, forward_step(): value_acc.at[flat_ids].add(part_v)  19.3 us
    ppermute x2, waiting for transfers between devices, shifted(): lax.ppermute(value, axis, [(i, (i + by) % devices) for i in range(devices)])  17.6 us
    all_to_all x1, starting transfers between devices, per_device(): lax.all_to_all(grad_v, 'head', split_axis=0, concat_axis=1, tiled=True)  12.7 us
    sub x4, matrix products, forward_step(): exp_scores = jnp.exp(scores - row_top)  12.1 us
    ppermute x2, starting transfers between devices, shifted(): lax.ppermute(value, axis, [(i, (i + by) % devices) for i in range(devices)])  11.7 us
  transfers between devices with their start and end apart: 11, of which 8 were waited for; matrix products, arithmetic and copies ran while one was open for 5% of the time, Pallas kernels for 0%

commit v1 on v0

v1 whole, which is shorter than its diff:
```python
import functools

import jax
import jax.numpy as jnp
from jax import lax
from jax.experimental import pallas as pl
from jax.experimental.pallas import tpu as pltpu
from jax.sharding import PartitionSpec as P

HD = 64
QB = 128
NNB = 8
MESH = pl.DeviceIdType.MESH
BF16 = jnp.bfloat16
F32 = jnp.float32


def kernel(
    n,
    meta,
    q_ref,
    k_ref,
    v_ref,
    d_ref,
    gq_ref,
    gk_ref,
    gv_ref,
    kv_send,
    qd_send,
    kv_win,
    kt_win,
    qd_all,
    st,
    w,
    parts,
    run,
    dq_send,
    dq_recv,
    part_send,
    part_recv,
    out_send,
    out_recv,
    kv_ss,
    kv_rs,
    fw_ss,
    fw_rs,
    qd_ss,
    qd_rs,
    dq_ss,
    dq_rs,
    pt_ss,
    pt_rs,
    ot_ss,
    ot_rs,
):
    blk, me = lax.axis_index("blk"), lax.axis_index("head")
    nblk = lax.axis_size("blk")
    before, after = lax.rem(blk + nblk - 1, nblk), lax.rem(blk + 1, nblk)
    pairs = n * NNB
    at_order, at_keep, at_last, at_has = pairs, 2 * pairs, 3 * pairs, 3 * pairs + 3 * n

    def peer(t):
        return lax.rem(me + t, n)

    def source(t):
        return lax.rem(me - t + n, n)

    def remote(src, dst, ss, rs, b, h):
        return pltpu.make_async_remote_copy(
            src_ref=src, dst_ref=dst, send_sem=ss, recv_sem=rs, device_id={"blk": b, "head": h}, device_id_type=MESH
        )

    def kv_copy(to):
        return remote(kv_send.at[to], kv_win.at[n + me], kv_ss.at[to], kv_rs.at[me], blk, to)

    def kv_arrival(src):
        return remote(kv_send.at[src], kv_win.at[n + src], kv_ss.at[src], kv_rs.at[src], blk, src)

    def qd_copy(to):
        return remote(qd_send.at[to], qd_all.at[me], qd_ss.at[to], qd_rs.at[me], blk, to)

    def qd_arrival(src):
        return remote(qd_send.at[src], qd_all.at[src], qd_ss.at[src], qd_rs.at[src], blk, src)

    def fw_copy(side, i):
        dst = kv_win.at[i] if side == 0 else kv_win.at[2 * n + i]
        return remote(
            kv_win.at[n + i], dst, fw_ss.at[side, i], fw_rs.at[side, i], after if side == 0 else before, me
        )

    def pt_copy(side, i):
        return remote(
            part_send.at[side, i],
            part_recv.at[side, i],
            pt_ss.at[side, i],
            pt_rs.at[side, i],
            before if side == 0 else after,
            me,
        )

    def dq_copy(to):
        rows = pl.ds(pl.multiple_of(me * HD, HD), HD)
        return remote(dq_send.at[to], dq_recv.at[rows], dq_ss.at[to], dq_rs.at[me], blk, to)

    def dq_arrival(src):
        rows = pl.ds(pl.multiple_of(src * HD, HD), HD)
        return remote(dq_send.at[src], dq_recv.at[rows], dq_ss.at[src], dq_rs.at[src], blk, src)

    def ot_copy(to):
        return remote(out_send.at[to], out_recv.at[me], ot_ss.at[to], ot_rs.at[me], blk, to)

    def ot_arrival(src):
        return remote(out_send.at[src], out_recv.at[src], ot_ss.at[src], ot_rs.at[src], blk, src)

    barrier = pltpu.get_barrier_semaphore()

    def greet(t, c):
        pl.semaphore_signal(barrier, inc=1, device_id={"head": peer(t)}, device_id_type=MESH)
        return c

    lax.fori_loop(1, n, greet, 0)
    pl.semaphore_signal(barrier, inc=1, device_id={"blk": before}, device_id_type=MESH)
    pl.semaphore_signal(barrier, inc=1, device_id={"blk": after}, device_id_type=MESH)

    def pack(a_ref, b_ref, to_ref, scale):
        for p in range(n // 2):
            cols = slice(2 * HD * p, 2 * HD * (p + 1))
            a, b = a_ref[:, cols], b_ref[:, cols]
            if scale is not None:
                a = (a.astype(F32) * scale).astype(BF16)
            to_ref[2 * p] = jnp.concatenate([a[:, :HD], b[:, :HD]], axis=1)
            to_ref[2 * p + 1] = jnp.concatenate([a[:, HD:], b[:, HD:]], axis=1)

    pack(k_ref, v_ref, kv_send, None)
    kv_win[n + me] = kv_send[me]
    pl.semaphore_wait(barrier, n + 1)

    def send_kv(t, c):
        kv_copy(peer(t)).start()
        return c

    lax.fori_loop(1, n, send_kv, 0)
    pack(q_ref, d_ref, qd_send, HD**-0.5)
    qd_all[me] = qd_send[me]

    def send_qd(t, c):
        qd_copy(peer(t)).start()
        return c

    lax.fori_loop(1, n, send_qd, 0)

    def turn(j):
        kt_win[j] = kv_win[j].T[:HD]

    def forward(t, c):
        i = source(t)

        @pl.when(t > 0)
        def _():
            kv_arrival(i).wait_recv()

        fw_copy(0, i).start()
        fw_copy(1, i).start()
        turn(n + i)
        return c

    lax.fori_loop(0, n, forward, 0)

    def window(t, c):
        i = source(t)
        fw_copy(0, i).wait_recv()
        turn(i)
        fw_copy(1, i).wait_recv()
        turn(2 * n + i)
        return c

    lax.fori_loop(0, n, window, 0)

    lane = lax.broadcasted_iota(jnp.int32, (QB, 2 * HD), 1)

    def fold(x, op):
        return op(x.reshape(QB // 8, 8, QB), axis=0)

    def query(t, c):
        i = source(t)

        @pl.when(t > 0)
        def _():
            qd_arrival(i).wait_recv()

        qd = qd_all[i]
        zero = jnp.zeros_like(qd)
        qd2 = jnp.concatenate([jnp.where(lane < HD, qd, zero), jnp.where(lane < HD, zero, qd)], axis=0)
        ids = [meta[i * NNB + s] for s in range(NNB)]
        top = None
        for s in range(NNB):
            r = lax.dot_general(
                kv_win[ids[s]], qd2, (((1,), (1,)), ((), ())), preferred_element_type=F32
            )
            st[s] = r
            m = fold(r[:, :QB], jnp.max)
            top = m if top is None else jnp.maximum(top, m)
        top = jnp.max(top, axis=0, keepdims=True)
        total = jnp.zeros((8, QB), F32)
        delta = jnp.zeros((8, QB), F32)
        for s in range(NNB):
            e = jnp.exp(st[s, :, :QB] - top)
            total += fold(e, jnp.sum)
            delta += fold(e * st[s, :, QB:], jnp.sum)
            st[s, :, :QB] = e
        inv = 1.0 / jnp.sum(total, axis=0, keepdims=True)
        delta = jnp.sum(delta, axis=0, keepdims=True) * inv
        for s in range(NNB):
            p = st[s, :, :QB] * inv
            ds = p * (st[s, :, QB:] - delta)
            w[s * QB : (s + 1) * QB, :QB] = ds.astype(BF16)
            w[s * QB : (s + 1) * QB, QB:] = p.astype(BF16)
        dqt = jnp.zeros((HD, QB), F32)
        for s in range(0, NNB, 2):
            kt = jnp.concatenate([kt_win[ids[s]], kt_win[ids[s + 1]]], axis=1)
            dqt += jnp.dot(kt, w[s * QB : (s + 2) * QB, :QB], preferred_element_type=F32)
        dqt = (dqt * HD**-0.5).astype(BF16)
        dq_send[i] = dqt

        @pl.when(t > 0)
        def _():
            dq_copy(i).start()

        @pl.when(t == 0)
        def _():
            dq_recv[pl.ds(pl.multiple_of(me * HD, HD), HD)] = dqt

        for s in range(NNB):
            parts[i * NNB + s] = jnp.dot(
                w[s * QB : (s + 1) * QB, :], qd2, preferred_element_type=F32
            )
        return c

    lax.fori_loop(0, n, query, 0)

    def add(e, acc):
        x = parts[meta[at_order + e]]
        acc = x + jnp.where(meta[at_keep + e] > 0, acc, 0.0)
        run[e] = acc
        return acc

    lax.fori_loop(0, pairs, add, jnp.zeros((QB, 2 * HD), F32))

    def summed(j):
        return jnp.where(meta[at_has + j] > 0, run[meta[at_last + j]], 0.0)

    def share(t, c):
        i = peer(t)
        part_send[0, i] = summed(i).astype(BF16)
        pt_copy(0, i).start()
        part_send[1, i] = summed(2 * n + i).astype(BF16)
        pt_copy(1, i).start()
        return c

    lax.fori_loop(1, n + 1, share, 0)

    def gather_dq(t, c):
        dq_arrival(source(t)).wait_recv()
        return c

    lax.fori_loop(1, n, gather_dq, 0)
    for p in range(n // 2):
        cols = slice(2 * HD * p, 2 * HD * (p + 1))
        gq_ref[:, cols] = dq_recv[cols].T

    def home(t, c):
        i = peer(t)
        pt_copy(0, i).wait_recv()
        pt_copy(1, i).wait_recv()
        x = summed(n + i) + part_recv[0, i].astype(F32) + part_recv[1, i].astype(F32)
        out_send[i] = x.astype(BF16)

        @pl.when(t < n)
        def _():
            ot_copy(i).start()

        @pl.when(t == n)
        def _():
            out_recv[me] = x.astype(BF16)

        return c

    lax.fori_loop(1, n + 1, home, 0)

    def gather_out(t, c):
        ot_arrival(source(t)).wait_recv()
        return c

    lax.fori_loop(1, n, gather_out, 0)
    for p in range(n // 2):
        cols = slice(2 * HD * p, 2 * HD * (p + 1))
        a, b = out_recv[2 * p], out_recv[2 * p + 1]
        gk_ref[:, cols] = jnp.concatenate([a[:, :HD], b[:, :HD]], axis=1)
        gv_ref[:, cols] = jnp.concatenate([a[:, HD:], b[:, HD:]], axis=1)

    def drain(t, c):
        to = peer(t)
        kv_copy(to).wait_send()
        qd_copy(to).wait_send()
        dq_copy(to).wait_send()
        ot_copy(to).wait_send()
        return c

    lax.fori_loop(1, n, drain, 0)

    def drain_sides(i, c):
        for side in (0, 1):
            fw_copy(side, i).wait_send()
            pt_copy(side, i).wait_send()
        return c

    lax.fori_loop(0, n, drain_sides, 0)


def per_device(query_rows, key_rows, value_rows, out_grad, block_pairs):
    n = lax.axis_size("head")
    pairs = n * NNB
    place = lax.axis_index("blk")
    own = lax.dynamic_slice_in_dim(block_pairs, place * n, n, 0).reshape(pairs)
    ids = (own - (place - 1) * n) % (n * lax.axis_size("blk"))
    e = jnp.arange(pairs, dtype=jnp.int32)
    less = (ids[None, :] < ids[:, None]) | ((ids[None, :] == ids[:, None]) & (e[None, :] < e[:, None]))
    rank = jnp.sum(less.astype(jnp.int32), axis=1)
    at = rank[None, :] == e[:, None]
    order = jnp.sum(jnp.where(at, e[None, :], 0), axis=1)
    same = (ids[None, :] == ids[:, None]) & (e[None, :] < e[:, None])
    going_on = jnp.any(same, axis=1).astype(jnp.int32)
    keep = jnp.sum(jnp.where(at, going_on[None, :], 0), axis=1)
    j = jnp.arange(3 * n, dtype=jnp.int32)
    upto = jnp.sum((ids[None, :] <= j[:, None]).astype(jnp.int32), axis=1)
    has = jnp.any(ids[None, :] == j[:, None], axis=1).astype(jnp.int32)
    meta = jnp.concatenate([ids, order, keep, jnp.maximum(upto - 1, 0), has]).astype(jnp.int32)

    rows = jax.ShapeDtypeStruct((QB, n * HD), BF16)
    tile = (QB, 2 * HD)
    dma = pltpu.SemaphoreType.DMA
    vmem = pl.BlockSpec(memory_space=pltpu.VMEM)
    return pl.pallas_call(
        functools.partial(kernel, n),
        out_shape=(rows, rows, rows),
        in_specs=[pl.BlockSpec(memory_space=pltpu.SMEM)] + [vmem] * 4,
        out_specs=(vmem, vmem, vmem),
        scratch_shapes=[
            pltpu.VMEM((n,) + tile, BF16),
            pltpu.VMEM((n,) + tile, BF16),
            pltpu.VMEM((3 * n,) + tile, BF16),
            pltpu.VMEM((3 * n, HD, QB), BF16),
            pltpu.VMEM((n,) + tile, BF16),
            pltpu.VMEM((NNB, QB, 2 * QB), F32),
            pltpu.VMEM((NNB * QB, 2 * QB), BF16),
            pltpu.VMEM((pairs,) + tile, F32),
            pltpu.VMEM((pairs,) + tile, F32),
            pltpu.VMEM((n, HD, QB), BF16),
            pltpu.VMEM((n * HD, QB), BF16),
            pltpu.VMEM((2, n) + tile, BF16),
            pltpu.VMEM((2, n) + tile, BF16),
            pltpu.VMEM((n,) + tile, BF16),
            pltpu.VMEM((n,) + tile, BF16),
            dma((n,)),
            dma((n,)),
            dma((2, n)),
            dma((2, n)),
            dma((n,)),
            dma((n,)),
            dma((n,)),
            dma((n,)),
            dma((2, n)),
            dma((2, n)),
            dma((n,)),
            dma((n,)),
        ],
        compiler_params=pltpu.CompilerParams(
            collective_id=0, has_side_effects=True, vmem_limit_bytes=48 * 1024 * 1024
        ),
    )(meta, query_rows, key_rows, value_rows, out_grad)


def solution(mesh):
    rows = P(("blk", "head"), None)
    return jax.shard_map(
        per_device,
        mesh=mesh,
        in_specs=(rows, rows, rows, rows, P()),
        out_specs=(rows, rows, rows),
        check_vma=False,
    )
```

time: 290 us -> 97.1 us (0.33)
  the two profiles are of different devices: /device:TPU:72 before, /device:TPU:64 now
where the time goes in v1:
time: 97.1 us; the launch traced here: 96.8 us
  Pallas kernels  88.5 us (91%)
  local copies, waits for them, and re-layouts  6.16 us (6%)
  other arithmetic  1.47 us (2%)
    pallas_call x1, Pallas kernels, per_device(): pl.pallas_call(functools.partial(kernel, n), out_shape=(rows, rows, rows)...  88.5 us
    unnamed x11, local copies, waits for them, and re-layouts  5.92 us

profile of v1, /device:TPU:64, one launch (start us, length us, event | category | flops | bytes accessed | tf_op | source)
XLA Modules:
  0.0 96.8 jit_solution(449921656711389438)
XLA Ops:
  0.6 0.8 dynamic-slice_subtract_fusion
  1.4 0.1 copy.10
  1.5 0.1 sub.27
  1.6 0.1 fusion.2
  1.7 0.1 convert_reduce_fusion.1
  1.8 0.2 fusion.1
  2.0 0.2 convert_reduce_fusion
  2.2 0.1 select_reduce_fusion
  2.3 0.1 concatenate.3.meta
  2.4 0.0 copy-start
  2.4 1.0 copy-done
  3.4 0.0 copy-start.1
  3.4 0.9 copy-done.1
  4.3 0.0 copy-start.2
  4.3 0.9 copy-done.2
  5.3 0.0 copy-start.3
  5.3 0.9 copy-done.3
  6.2 88.5 %shard_map.76 = (bf16[128,1024]{1,0:T(8,128)(2,1)S(1)}, bf16[128,1024]{1,0:T(8,128)(2,1)S(1)}, bf16[128,1024]{1,0:T(8,128)(2,1)S(1)}) custom-call(s32[480]{0:T(512)S(1)} %concatenate.3.meta, bf16[128,1024]{1,0:T(8,128)(2,1)S(1)} %copy-done, bf16[128,1024]{1,0:T(8,128)(2,1)S(1)} %copy-done.1, bf16[128,1024]{1,0:T(8,128)(2,1)S(1)} %copy-done.2, ...), custom_call_target="tpu_custom_call" | custom-call | tf_op jit(solution)/shard_map/pallas_call | solution.py:343
  94.7 0.7 copy.14
  95.4 0.7 copy.15
  96.1 0.7 copy.16
  (4 shorter events, 0.0 us)
Async XLA Ops:
  2.4 1.0 copy-start
  3.4 0.9 copy-start.1
  4.3 0.9 copy-start.2
  5.3 0.9 copy-start.3

commit v2 on v1

--- a/solution.py
+++ b/solution.py
@@ -18,20 +18,28 @@
 def kernel(
     n,
     meta,
+    q_hbm,
+    k_hbm,
+    v_hbm,
+    d_hbm,
+    gq_ref,
+    gk_ref,
+    gv_ref,
     q_ref,
     k_ref,
     v_ref,
     d_ref,
-    gq_ref,
-    gk_ref,
-    gv_ref,
     kv_send,
     qd_send,
     kv_win,
     kt_win,
     qd_all,
-    st,
-    w,
+    st0,
+    st1,
+    tops0,
+    tops1,
+    w0,
+    w1,
     parts,
     run,
     dq_send,
@@ -40,6 +48,7 @@
     part_recv,
     out_send,
     out_recv,
+    in_sems,
     kv_ss,
     kv_rs,
     fw_ss,
@@ -58,12 +67,20 @@
     before, after = lax.rem(blk + nblk - 1, nblk), lax.rem(blk + 1, nblk)
     pairs = n * NNB
     at_order, at_keep, at_last, at_has = pairs, 2 * pairs, 3 * pairs, 3 * pairs + 3 * n
+    nz = n // 2
+    my_y, my_z = me // nz, lax.rem(me, nz)
+
+    def offset(t):
+        k = t // 2
+        return lax.rem(t, 2), (k + 1) // 2 * (2 * lax.rem(k, 2) - 1)
 
     def peer(t):
-        return lax.rem(me + t, n)
+        dy, dz = offset(t)
+        return lax.rem(my_y + dy, 2) * nz + lax.rem(my_z + dz + nz, nz)
 
     def source(t):
-        return lax.rem(me - t + n, n)
+        dy, dz = offset(t)
+        return lax.rem(my_y + dy, 2) * nz + lax.rem(my_z - dz + nz, nz)
 
     def remote(src, dst, ss, rs, b, h):
         return pltpu.make_async_remote_copy(
@@ -112,6 +129,10 @@
     def ot_arrival(src):
         return remote(out_send.at[src], out_recv.at[src], ot_ss.at[src], ot_rs.at[src], blk, src)
 
+    def read(i):
+        src, dst = (k_hbm, v_hbm, q_hbm, d_hbm)[i], (k_ref, v_ref, q_ref, d_ref)[i]
+        return pltpu.make_async_copy(src, dst, in_sems.at[i])
+
     barrier = pltpu.get_barrier_semaphore()
 
     def greet(t, c):
@@ -121,6 +142,8 @@
     lax.fori_loop(1, n, greet, 0)
     pl.semaphore_signal(barrier, inc=1, device_id={"blk": before}, device_id_type=MESH)
     pl.semaphore_signal(barrier, inc=1, device_id={"blk": after}, device_id_type=MESH)
+    for i in range(4):
+        read(i).start()
 
     def pack(a_ref, b_ref, to_ref, scale):
         for p in range(n // 2):
@@ -131,6 +154,8 @@
             to_ref[2 * p] = jnp.concatenate([a[:, :HD], b[:, :HD]], axis=1)
             to_ref[2 * p + 1] = jnp.concatenate([a[:, HD:], b[:, HD:]], axis=1)
 
+    read(0).wait()
+    read(1).wait()
     pack(k_ref, v_ref, kv_send, None)
     kv_win[n + me] = kv_send[me]
     pl.semaphore_wait(barrier, n + 1)
@@ -140,14 +165,10 @@
         return c
 
     lax.fori_loop(1, n, send_kv, 0)
+    read(2).wait()
+    read(3).wait()
     pack(q_ref, d_ref, qd_send, HD**-0.5)
     qd_all[me] = qd_send[me]
-
-    def send_qd(t, c):
-        qd_copy(peer(t)).start()
-        return c
-
-    lax.fori_loop(1, n, send_qd, 0)
 
     def turn(j):
         kt_win[j] = kv_win[j].T[:HD]
@@ -158,6 +179,7 @@
         @pl.when(t > 0)
         def _():
             kv_arrival(i).wait_recv()
+            qd_copy(peer(t)).start()
 
         fw_copy(0, i).start()
         fw_copy(1, i).start()
@@ -181,17 +203,14 @@
     def fold(x, op):
         return op(x.reshape(QB // 8, 8, QB), axis=0)
 
-    def query(t, c):
-        i = source(t)
-
-        @pl.when(t > 0)
-        def _():
-            qd_arrival(i).wait_recv()
-
+    def operands(i):
         qd = qd_all[i]
         zero = jnp.zeros_like(qd)
         qd2 = jnp.concatenate([jnp.where(lane < HD, qd, zero), jnp.where(lane < HD, zero, qd)], axis=0)
-        ids = [meta[i * NNB + s] for s in range(NNB)]
+        return qd2, [meta[i * NNB + s] for s in range(NNB)]
+
+    def scores(i, st, tops):
+        qd2, ids = operands(i)
         top = None
         for s in range(NNB):
             r = lax.dot_general(
@@ -200,7 +219,11 @@
             st[s] = r
             m = fold(r[:, :QB], jnp.max)
             top = m if top is None else jnp.maximum(top, m)
-        top = jnp.max(top, axis=0, keepdims=True)
+        tops[...] = top
+
+    def grads(i, st, tops, w):
+        qd2, ids = operands(i)
+        top = jnp.max(tops[...], axis=0, keepdims=True)
         total = jnp.zeros((8, QB), F32)
         delta = jnp.zeros((8, QB), F32)
         for s in range(NNB):
@@ -219,24 +242,36 @@
         for s in range(0, NNB, 2):
             kt = jnp.concatenate([kt_win[ids[s]], kt_win[ids[s + 1]]], axis=1)
             dqt += jnp.dot(kt, w[s * QB : (s + 2) * QB, :QB], preferred_element_type=F32)
-        dqt = (dqt * HD**-0.5).astype(BF16)
-        dq_send[i] = dqt
-
-        @pl.when(t > 0)
-        def _():
-            dq_copy(i).start()
-
-        @pl.when(t == 0)
-        def _():
-            dq_recv[pl.ds(pl.multiple_of(me * HD, HD), HD)] = dqt
-
+        dq_send[i] = (dqt * HD**-0.5).astype(BF16)
         for s in range(NNB):
             parts[i * NNB + s] = jnp.dot(
                 w[s * QB : (s + 1) * QB, :], qd2, preferred_element_type=F32
             )
-        return c
-
-    lax.fori_loop(0, n, query, 0)
+
+    scores(me, st0, tops0)
+
+    def query(u, c):
+        i0, i1, i2 = source(2 * u), source(2 * u + 1), source(lax.rem(2 * u + 2, n))
+        qd_arrival(i1).wait_recv()
+
+        @pl.when(2 * u + 2 < n)
+        def _():
+            qd_arrival(i2).wait_recv()
+
+        scores(i1, st1, tops1)
+        grads(i0, st0, tops0, w0)
+        scores(i2, st0, tops0)
+        grads(i1, st1, tops1, w1)
+
+        @pl.when(u > 0)
+        def _():
+            dq_copy(i0).start()
+
+        dq_copy(i1).start()
+        return c
+
+    lax.fori_loop(0, n // 2, query, 0)
+    dq_recv[pl.ds(pl.multiple_of(me * HD, HD), HD)] = dq_send[me]
 
     def add(e, acc):
         x = parts[meta[at_order + e]]
@@ -250,7 +285,7 @@
         return jnp.where(meta[at_has + j] > 0, run[meta[at_last + j]], 0.0)
 
     def share(t, c):
-        i = peer(t)
+        i = peer(n - t)
         part_send[0, i] = summed(i).astype(BF16)
         pt_copy(0, i).start()
         part_send[1, i] = summed(2 * n + i).astype(BF16)
@@ -269,7 +304,7 @@
         gq_ref[:, cols] = dq_recv[cols].T
 
     def home(t, c):
-        i = peer(t)
+        i = peer(n - t)
         pt_copy(0, i).wait_recv()
         pt_copy(1, i).wait_recv()
         x = summed(n + i) + part_recv[0, i].astype(F32) + part_recv[1, i].astype(F32)
@@ -343,15 +378,23 @@
     return pl.pallas_call(
         functools.partial(kernel, n),
         out_shape=(rows, rows, rows),
-        in_specs=[pl.BlockSpec(memory_space=pltpu.SMEM)] + [vmem] * 4,
+        in_specs=[pl.BlockSpec(memory_space=pltpu.SMEM)] + [pl.BlockSpec(memory_space=pl.ANY)] * 4,
         out_specs=(vmem, vmem, vmem),
         scratch_shapes=[
+            pltpu.VMEM((QB, n * HD), BF16),
+            pltpu.VMEM((QB, n * HD), BF16),
+            pltpu.VMEM((QB, n * HD), BF16),
+            pltpu.VMEM((QB, n * HD), BF16),
             pltpu.VMEM((n,) + tile, BF16),
             pltpu.VMEM((n,) + tile, BF16),
             pltpu.VMEM((3 * n,) + tile, BF16),
             pltpu.VMEM((3 * n, HD, QB), BF16),
             pltpu.VMEM((n,) + tile, BF16),
             pltpu.VMEM((NNB, QB, 2 * QB), F32),
+            pltpu.VMEM((NNB, QB, 2 * QB), F32),
+            pltpu.VMEM((8, QB), F32),
+            pltpu.VMEM((8, QB), F32),
+            pltpu.VMEM((NNB * QB, 2 * QB), BF16),
             pltpu.VMEM((NNB * QB, 2 * QB), BF16),
             pltpu.VMEM((pairs,) + tile, F32),
             pltpu.VMEM((pairs,) + tile, F32),
@@ -361,6 +404,7 @@
             pltpu.VMEM((2, n) + tile, BF16),
             pltpu.VMEM((n,) + tile, BF16),
             pltpu.VMEM((n,) + tile, BF16),
+            dma((4,)),
             dma((n,)),
             dma((n,)),
             dma((2, n)),
@@ -375,7 +419,7 @@
             dma((n,)),
         ],
         compiler_params=pltpu.CompilerParams(
-            collective_id=0, has_side_effects=True, vmem_limit_bytes=48 * 1024 * 1024
+            collective_id=0, has_side_effects=True, vmem_limit_bytes=60 * 1024 * 1024
         ),
     )(meta, query_rows, key_rows, value_rows, out_grad)
 

time: 97.1 us -> 81.8 us (0.84)
  the two profiles are of different devices: /device:TPU:64 before, /device:TPU:8 now
where the time goes in v2:
time: 81.8 us; the launch traced here: 81.6 us
  Pallas kernels  75.1 us (92%)
  local copies, waits for them, and re-layouts  4.29 us (5%)
  other arithmetic  1.47 us (2%)
    pallas_call x1, Pallas kernels, per_device(): pl.pallas_call(functools.partial(kernel, n), out_shape=(rows, rows, rows)...  75.1 us
    unnamed x7, local copies, waits for them, and re-layouts  3.46 us

profile of v2, /device:TPU:8, one launch (start us, length us, event | category | flops | bytes accessed | tf_op | source)
XLA Modules:
  0.0 81.6 jit_solution(928139626350249031)
XLA Ops:
  0.6 0.8 dynamic-slice_subtract_fusion
  1.4 0.1 copy.10
  1.5 0.1 sub.27
  1.6 0.1 fusion.2
  1.7 0.1 convert_reduce_fusion.1
  1.8 0.2 fusion.1
  2.0 0.2 convert_reduce_fusion
  2.2 0.1 select_reduce_fusion
  2.3 0.7 concatenate.3.meta
  3.0 75.1 %shard_map.76 = (bf16[128,1024]{1,0:T(8,128)(2,1)}, bf16[128,1024]{1,0:T(8,128)(2,1)}, bf16[128,1024]{1,0:T(8,128)(2,1)}) custom-call(s32[480]{0:T(512)} %concatenate.3.meta, bf16[128,1024]{1,0:T(8,128)(2,1)} %q_hbm.1, bf16[128,1024]{1,0:T(8,128)(2,1)} %k_hbm.1, bf16[128,1024]{1,0:T(8,128)(2,1)} %v_hbm.1, bf16[128,1024]{1,0:T(8,128)(2,1)} %d_hbm.1), custom_call_target="tpu_custom_call" | custom-call | tf_op jit(solution)/shard_map/pallas_call | solution.py:378
  78.1 0.0 copy-start.1
  78.1 1.7 %copy.14 = bf16[128,1024]{1,0:T(8,128)(2,1)} copy(bf16[128,1024]{1,0:T(8,128)(2,1)} %get-tuple-element.8) | data formatting | bytes 524288
  79.8 0.0 copy-done.1
  79.8 0.0 copy-start
  79.8 0.7 copy.15
  80.5 0.3 copy-done
  80.9 0.7 copy.16
  (4 shorter events, 0.0 us)
Async XLA Ops:
  78.1 1.7 %copy-start.1 = (bf16[128,1024]{1,0:T(8,128)(2,1)S(1)}, bf16[128,1024]{1,0:T(8,128)(2,1)}, u32[]{:S(2)}) copy-start(bf16[128,1024]{1,0:T(8,128)(2,1)} %get-tuple-element.9) | copy-start | bytes 786436
  79.8 1.0 %copy-start = (bf16[128,1024]{1,0:T(8,128)(2,1)S(1)}, bf16[128,1024]{1,0:T(8,128)(2,1)}, u32[]{:S(2)}) copy-start(bf16[128,1024]{1,0:T(8,128)(2,1)} %get-tuple-element.10) | copy-start | bytes 786436

commit v3 on v2

--- a/solution.py
+++ b/solution.py
@@ -22,9 +22,8 @@
     k_hbm,
     v_hbm,
     d_hbm,
-    gq_ref,
-    gk_ref,
-    gv_ref,
+    dq_recv,
+    out_recv,
     q_ref,
     k_ref,
     v_ref,
@@ -43,11 +42,9 @@
     parts,
     run,
     dq_send,
-    dq_recv,
     part_send,
     part_recv,
     out_send,
-    out_recv,
     in_sems,
     kv_ss,
     kv_rs,
@@ -179,7 +176,6 @@
         @pl.when(t > 0)
         def _():
             kv_arrival(i).wait_recv()
-            qd_copy(peer(t)).start()
 
         fw_copy(0, i).start()
         fw_copy(1, i).start()
@@ -187,6 +183,12 @@
         return c
 
     lax.fori_loop(0, n, forward, 0)
+
+    def send_qd(t, c):
+        qd_copy(peer(t)).start()
+        return c
+
+    lax.fori_loop(1, n, send_qd, 0)
 
     def window(t, c):
         i = source(t)
@@ -299,9 +301,6 @@
         return c
 
     lax.fori_loop(1, n, gather_dq, 0)
-    for p in range(n // 2):
-        cols = slice(2 * HD * p, 2 * HD * (p + 1))
-        gq_ref[:, cols] = dq_recv[cols].T
 
     def home(t, c):
         i = peer(n - t)
@@ -327,11 +326,6 @@
         return c
 
     lax.fori_loop(1, n, gather_out, 0)
-    for p in range(n // 2):
-        cols = slice(2 * HD * p, 2 * HD * (p + 1))
-        a, b = out_recv[2 * p], out_recv[2 * p + 1]
-        gk_ref[:, cols] = jnp.concatenate([a[:, :HD], b[:, :HD]], axis=1)
-        gv_ref[:, cols] = jnp.concatenate([a[:, HD:], b[:, HD:]], axis=1)
 
     def drain(t, c):
         to = peer(t)
@@ -350,6 +344,15 @@
         return c
 
     lax.fori_loop(0, n, drain_sides, 0)
+
+
+def unpack(n, dq_ref, out_ref, gq_ref, gk_ref, gv_ref):
+    for p in range(n // 2):
+        cols = slice(2 * HD * p, 2 * HD * (p + 1))
+        gq_ref[:, cols] = dq_ref[cols].T
+        a, b = out_ref[2 * p], out_ref[2 * p + 1]
+        gk_ref[:, cols] = jnp.concatenate([a[:, :HD], b[:, :HD]], axis=1)
+        gv_ref[:, cols] = jnp.concatenate([a[:, HD:], b[:, HD:]], axis=1)
 
 
 def per_device(query_rows, key_rows, value_rows, out_grad, block_pairs):
@@ -375,11 +378,14 @@
     tile = (QB, 2 * HD)
     dma = pltpu.SemaphoreType.DMA
     vmem = pl.BlockSpec(memory_space=pltpu.VMEM)
-    return pl.pallas_call(
+    arrived = pl.pallas_call(
         functools.partial(kernel, n),
-        out_shape=(rows, rows, rows),
+        out_shape=(
+            jax.ShapeDtypeStruct((n * HD, QB), BF16),
+            jax.ShapeDtypeStruct((n,) + tile, BF16),
+        ),
         in_specs=[pl.BlockSpec(memory_space=pltpu.SMEM)] + [pl.BlockSpec(memory_space=pl.ANY)] * 4,
-        out_specs=(vmem, vmem, vmem),
+        out_specs=(vmem, vmem),
         scratch_shapes=[
             pltpu.VMEM((QB, n * HD), BF16),
             pltpu.VMEM((QB, n * HD), BF16),
@@ -399,10 +405,8 @@
             pltpu.VMEM((pairs,) + tile, F32),
             pltpu.VMEM((pairs,) + tile, F32),
             pltpu.VMEM((n, HD, QB), BF16),
-            pltpu.VMEM((n * HD, QB), BF16),
             pltpu.VMEM((2, n) + tile, BF16),
             pltpu.VMEM((2, n) + tile, BF16),
-            pltpu.VMEM((n,) + tile, BF16),
             pltpu.VMEM((n,) + tile, BF16),
             dma((4,)),
             dma((n,)),
@@ -422,6 +426,12 @@
             collective_id=0, has_side_effects=True, vmem_limit_bytes=60 * 1024 * 1024
         ),
     )(meta, query_rows, key_rows, value_rows, out_grad)
+    return pl.pallas_call(
+        functools.partial(unpack, n),
+        out_shape=(rows, rows, rows),
+        in_specs=[vmem, vmem],
+        out_specs=(vmem, vmem, vmem),
+    )(*arrived)
 
 
 def solution(mesh):

time: 81.8 us -> 79.1 us (0.967)
  the two profiles are of different devices: /device:TPU:8 before, /device:TPU:7 now
where the time goes in v3:
time: 79.1 us; the launch traced here: 78.8 us
  Pallas kernels  75.8 us (96%)
  other arithmetic  1.47 us (2%)
  local copies, waits for them, and re-layouts  0.83 us (1%)
    pallas_call x1, Pallas kernels, per_device(): pl.pallas_call(functools.partial(kernel, n), out_shape=(jax.ShapeDtypeStr...  73.6 us
    pallas_call x1, Pallas kernels, per_device(): pl.pallas_call(functools.partial(unpack, n), out_shape=(rows, rows, rows)...  2.25 us

profile of v3, /device:TPU:7, one launch (start us, length us, event | category | flops | bytes accessed | tf_op | source)
XLA Modules:
  0.0 78.8 jit_solution(17009150580984228775)
XLA Ops:
  0.6 0.8 dynamic-slice_subtract_fusion
  1.4 0.1 copy.10
  1.5 0.1 sub.27
  1.6 0.1 fusion.2
  1.7 0.1 convert_reduce_fusion.1
  1.8 0.2 fusion.1
  2.0 0.2 convert_reduce_fusion
  2.2 0.1 select_reduce_fusion
  2.3 0.7 concatenate.3.meta
  3.0 73.6 %shard_map.76 = (bf16[1024,128]{1,0:T(8,128)(2,1)}, bf16[16,128,128]{2,1,0:T(8,128)(2,1)}) custom-call(s32[480]{0:T(512)} %concatenate.3.meta, bf16[128,1024]{1,0:T(8,128)(2,1)} %q_hbm.1, bf16[128,1024]{1,0:T(8,128)(2,1)} %k_hbm.1, bf16[128,1024]{1,0:T(8,128)(2,1)} %v_hbm.1, bf16[128,1024]{1,0:T(8,128)(2,1)} %d_hbm.1), custom_call_target="tpu_custom_call" | custom-call | tf_op jit(solution)/shard_map/pallas_call | solution.py:381
  76.6 2.3 %shard_map.77 = (bf16[128,1024]{1,0:T(8,128)(2,1)}, bf16[128,1024]{1,0:T(8,128)(2,1)}, bf16[128,1024]{1,0:T(8,128)(2,1)}) custom-call(bf16[1024,128]{1,0:T(8,128)(2,1)} %get-tuple-element.5.dq_ref, bf16[16,128,128]{2,1,0:T(8,128)(2,1)} %get-tuple-element.6.out_ref), custom_call_target="tpu_custom_call" | custom-call | tf_op jit(solution)/shard_map/pallas_call | solution.py:429
  (4 shorter events, 0.0 us)

commit v4 on v3

--- a/solution.py
+++ b/solution.py
@@ -300,7 +300,6 @@
         dq_arrival(source(t)).wait_recv()
         return c
 
-    lax.fori_loop(1, n, gather_dq, 0)
 
     def home(t, c):
         i = peer(n - t)
@@ -320,6 +319,7 @@
         return c
 
     lax.fori_loop(1, n + 1, home, 0)
+    lax.fori_loop(1, n, gather_dq, 0)
 
     def gather_out(t, c):
         ot_arrival(source(t)).wait_recv()

time: 79.1 us -> 79.6 us (level)
  the two profiles are of different devices: /device:TPU:7 before, /device:TPU:8 now
where the time goes in v4:
time: 79.6 us; the launch traced here: 79.4 us
  Pallas kernels  76.4 us (96%)
  other arithmetic  1.47 us (2%)
  local copies, waits for them, and re-layouts  0.83 us (1%)
    pallas_call x1, Pallas kernels, per_device(): pl.pallas_call(functools.partial(kernel, n), out_shape=(jax.ShapeDtypeStr...  74.1 us
    pallas_call x1, Pallas kernels, per_device(): pl.pallas_call(functools.partial(unpack, n), out_shape=(rows, rows, rows)...  2.25 us

profile of v4, /device:TPU:8, one launch (start us, length us, event | category | flops | bytes accessed | tf_op | source)
XLA Modules:
  0.0 79.4 jit_solution(11961298492535865841)
XLA Ops:
  0.6 0.8 dynamic-slice_subtract_fusion
  1.4 0.1 copy.10
  1.5 0.1 sub.27
  1.6 0.1 fusion.2
  1.7 0.1 convert_reduce_fusion.1
  1.8 0.2 fusion.1
  2.0 0.2 convert_reduce_fusion
  2.2 0.1 select_reduce_fusion
  2.3 0.7 concatenate.3.meta
  3.0 74.1 %shard_map.76 = (bf16[1024,128]{1,0:T(8,128)(2,1)}, bf16[16,128,128]{2,1,0:T(8,128)(2,1)}) custom-call(s32[480]{0:T(512)} %concatenate.3.meta, bf16[128,1024]{1,0:T(8,128)(2,1)} %q_hbm.1, bf16[128,1024]{1,0:T(8,128)(2,1)} %k_hbm.1, bf16[128,1024]{1,0:T(8,128)(2,1)} %v_hbm.1, bf16[128,1024]{1,0:T(8,128)(2,1)} %d_hbm.1), custom_call_target="tpu_custom_call" | custom-call | tf_op jit(solution)/shard_map/pallas_call | solution.py:381
  77.1 2.3 %shard_map.77 = (bf16[128,1024]{1,0:T(8,128)(2,1)}, bf16[128,1024]{1,0:T(8,128)(2,1)}, bf16[128,1024]{1,0:T(8,128)(2,1)}) custom-call(bf16[1024,128]{1,0:T(8,128)(2,1)} %get-tuple-element.5.dq_ref, bf16[16,128,128]{2,1,0:T(8,128)(2,1)} %get-tuple-element.6.out_ref), custom_call_target="tpu_custom_call" | custom-call | tf_op jit(solution)/shard_map/pallas_call | solution.py:429
  (4 shorter events, 0.0 us)
